TPU v7x, 256 devices: a whole 4x4x8 slice. The times are simulated.
256 devices in a mesh: dp: 32 (over z, x_hi, core), pipe: 8 (over y, x_lo).
Axes of the slice: x: 4 (x_hi: 2, x_lo: 2; x = x_hi * 2 + x_lo), y: 4, z: 8, core: 2. Of those that a mesh axis runs over, the one named last changes fastest.
Arguments:
- tokens: bfloat16 [98304, 4096], P(('dp', 'pipe')), may hold values from -24 to 24
- queries: bfloat16 [98304, 4096], P(('dp', 'pipe')), may hold values from -300 to 300, as said below
- kv_weight: bfloat16 [1024, 4096], P('pipe', 'dp'), may hold values from -0.09375 to 0.09375
- cotangent: bfloat16 [98304, 4096], P(('dp', 'pipe')), may hold values from -0.078125 to 0.078125
Outputs:
- attended: bfloat16 [98304, 4096], P(('dp', 'pipe'))
- kv_grad: float32 [1024, 4096], P('pipe', 'dp')
Inputs may be any that keep to these rules, and one draw needn't show every extreme that they name: `queries`: independent normal entries, a scale for each row.
All inputs are finite; a program needn't handle non-finite values.
Results may differ from a plain program's by a relative error of at most 0.02.
The roundings to bfloat16 on the way count: a program that leaves them out, or rounds other values in their place, can miss the bound.
Values may be sent and summed in bfloat16 or wider, within the bound.
A program may use at most 128 MiB of HBM per device.

v0:
```python
import jax
import jax.numpy as jnp
from jax import lax
from jax.sharding import PartitionSpec as P

HEADS = 32
KV_HEADS = 4
HEAD_DIM = 128


def group_pass(pieces):
    query_group, key_rows, value_rows, grad_group = pieces
    seq_len = key_rows.shape[0]
    scale_factor = 1.0 / HEAD_DIM**0.5
    scores = (
        jnp.einsum("sgd,td->gst", query_group, key_rows, preferred_element_type=jnp.float32)
        * scale_factor
    )
    causal = jnp.arange(seq_len)[:, None] >= jnp.arange(seq_len)[None, :]
    scores = jnp.where(causal, scores, jnp.float32(-1e30))
    row_max = jnp.max(scores, axis=-1, keepdims=True)
    expsum = jnp.exp(scores - row_max)
    probs_fp = expsum / jnp.sum(expsum, axis=-1, keepdims=True)
    probs_half = probs_fp.astype(jnp.bfloat16)
    output = jnp.einsum(
        "gst,td->sgd", probs_half, value_rows, preferred_element_type=jnp.float32
    ).astype(jnp.bfloat16)
    d_values = jnp.einsum("gst,sgd->td", probs_half, grad_group, preferred_element_type=jnp.float32)
    d_probs = jnp.einsum("sgd,td->gst", grad_group, value_rows, preferred_element_type=jnp.float32)
    inner = jnp.sum(probs_fp * d_probs, axis=-1, keepdims=True)
    d_scores = (probs_fp * (d_probs - inner) * scale_factor).astype(jnp.bfloat16)
    d_keys = jnp.einsum("gst,sgd->td", d_scores, query_group, preferred_element_type=jnp.float32)
    return (output, d_keys, d_values)


def attention_both(queries, key_value, cotangent):
    seq_len = queries.shape[0]
    groups = HEADS // KV_HEADS
    query_split = queries.reshape(seq_len, KV_HEADS, groups, HEAD_DIM).transpose(1, 0, 2, 3)
    grad_split = cotangent.reshape(seq_len, KV_HEADS, groups, HEAD_DIM).transpose(1, 0, 2, 3)
    key_split = (
        key_value[:, : KV_HEADS * HEAD_DIM].reshape(seq_len, KV_HEADS, HEAD_DIM).transpose(1, 0, 2)
    )
    value_split = (
        key_value[:, KV_HEADS * HEAD_DIM :].reshape(seq_len, KV_HEADS, HEAD_DIM).transpose(1, 0, 2)
    )
    outputs, d_keys, d_values = lax.map(
        group_pass, (query_split, key_split, value_split, grad_split)
    )
    attended = outputs.transpose(1, 0, 2, 3).reshape(seq_len, HEADS * HEAD_DIM)
    d_keys = d_keys.transpose(1, 0, 2).reshape(seq_len, KV_HEADS * HEAD_DIM)
    d_values = d_values.transpose(1, 0, 2).reshape(seq_len, KV_HEADS * HEAD_DIM)
    d_key_value = jnp.concatenate([d_keys, d_values], axis=1).astype(jnp.bfloat16)
    return (attended, d_key_value)


def on_device(tokens, queries, kv_weight, cotangent):
    block_rows, block_cols = kv_weight.shape
    dp_count = lax.axis_size("dp")
    pipe_count = lax.axis_size("pipe")
    gathered = lax.all_gather(kv_weight[None], ("dp", "pipe"), axis=0, tiled=True)
    whole_weight = gathered.reshape(dp_count, pipe_count, block_rows, block_cols)
    whole_weight = whole_weight.transpose(1, 2, 0, 3).reshape(
        pipe_count * block_rows, dp_count * block_cols
    )
    key_value = jnp.einsum(
        "sd,rd->sr", tokens, whole_weight, preferred_element_type=jnp.float32
    ).astype(jnp.bfloat16)
    attended, d_key_value = attention_both(queries, key_value, cotangent)
    full_grad = jnp.einsum("sr,sd->rd", d_key_value, tokens, preferred_element_type=jnp.float32)
    arranged = full_grad.reshape(pipe_count, block_rows, dp_count, block_cols)
    arranged = arranged.transpose(2, 0, 1, 3).reshape(
        dp_count * pipe_count * block_rows, block_cols
    )
    kv_grad = lax.psum_scatter(arranged, ("dp", "pipe"), scatter_dimension=0, tiled=True)
    return (attended, kv_grad)


def solution(mesh):
    placed = (
        P(("dp", "pipe"), None),
        P(("dp", "pipe"), None),
        P("pipe", "dp"),
        P(("dp", "pipe"), None),
    )
    return jax.shard_map(
        on_device,
        mesh=mesh,
        in_specs=placed,
        out_specs=(P(("dp", "pipe"), None), P("pipe", "dp")),
        check_vma=False,
    )
```

profile of v0, /device:TPU:10, one launch (start us, length us, event | category | flops | bytes accessed | tf_op | source)
XLA Modules:
  0.0 2160.2 jit_solution(6786675452485939237)
XLA Ops:
  7.2 0.0 copy-start
  7.2 0.0 all-gather.3.cloned.1.call-start
  7.2 0.7 all-gather.3.cloned.1.call-update
  7.9 0.0 reduce-scatter.2.cloned.1.call-start
  8.0 4.8 copy.17
  12.7 4.7 copy.18
  17.4 701.9 %all-gather.3.cloned.1.call-done = bf16[32768,128]{1,0:T(8,128)(2,1)} async-done(((bf16[128,128]{1,0:T(8,128)(2,1)}), bf16[32768,128]{1,0:T(8,128)(2,1)}) %all-gather.3.cloned.1.call-update) | async-done | bytes 8388624 | tf_op jit(solution)/shard_map/all_gather | solution.py:61
  719.3 12.0 copy.14
  731.4 0.0 copy-done
  731.4 6.3 fusion.58
  737.6 0.8 slice_bitcast_fusion
  738.5 0.1 copy.46
  738.5 1.9 copy.28
  740.4 75.5 %while.14 = (s32[]{:T(128)}, bf16[4,384,8,128]{1,3,2,0:T(8,128)(2,1)}, bf16[4,384,128]{1,2,0:T(8,128)(2,1)}, bf16[4,384,128]{1,2,0:T(8,128)(2,1)}, bf16[4,384,12...) while((s32[]{:T(128)}, ...), condition=%wide.region_4.5_spmd, body=%wide.region_0.4_spmd.sunk | while | flops 1530547968 | bytes 88343800 | solution.py:47
  740.5 1.9 fusion.94
  742.4 0.0 copy-start.1
  742.4 0.0 copy-start.3
  742.4 1.5 fusion.95
  744.0 0.0 copy-start.5
  744.0 0.3 copy-done.1
  744.3 0.1 copy-done.3
  744.3 0.8 fusion.99
  745.2 0.9 copy-done.5
  746.1 0.0 copy-done.2
  746.1 1.5 fusion.96
  747.6 0.0 copy-done.4
  747.6 3.0 fusion.97
  750.6 8.7 fusion.98
  759.3 1.9 fusion.94
  761.2 1.5 fusion.95
  762.8 0.3 copy-done.1
  763.1 0.1 copy-done.3
  763.2 0.8 fusion.99
  764.0 0.9 copy-done.5
  764.9 1.5 fusion.96
  766.4 0.0 copy-done.4
  766.4 3.0 fusion.97
  769.4 8.7 fusion.98
  778.2 1.9 fusion.94
  780.1 1.5 fusion.95
  781.7 0.3 copy-done.1
  782.0 0.1 copy-done.3
  782.0 0.8 fusion.99
  782.9 0.9 copy-done.5
  783.8 1.5 fusion.96
  785.3 0.0 copy-done.4
  785.3 3.0 fusion.97
  788.3 8.8 fusion.98
  797.1 1.9 fusion.94
  799.0 1.5 fusion.95
  800.6 0.3 copy-done.1
  800.9 0.1 copy-done.3
  801.0 0.8 fusion.99
  801.8 0.9 copy-done.5
  802.7 1.5 fusion.96
  804.2 3.0 fusion.97
  807.2 8.7 fusion.98
  815.9 5.6 convolution_bitcast_fusion
  821.6 6.8 copy.38
  828.4 6.8 bitcast_bitcast_fusion
  835.2 19.5 copy.24
  854.7 0.0 reduce-scatter.2.cloned.1.call-update
  854.8 4.6 copy.29
  859.4 1293.9 %reduce-scatter.2.cloned.1.call-done = f32[128,128]{1,0:T(8,128)} async-done(((f32[32768,128]{1,0:T(8,128)}), f32[128,128]{1,0:T(8,128)}) %reduce-scatter.2.cloned.1.call-update) | async-done | bytes 65552 | tf_op jit(solution)/shard_map/reduce_scatter | solution.py:75
  (28 shorter events, 0.2 us)
Async XLA Ops:
  7.2 724.2 %copy-start = (bf16[384,4096]{1,0:T(8,128)(2,1)S(1)}, bf16[384,4096]{1,0:T(8,128)(2,1)}, u32[]{:S(2)}) copy-start(bf16[384,4096]{1,0:T(8,128)(2,1)} %param.6) | copy-start | bytes 9437188
  7.2 712.2 %all-gather.3.cloned.1.call-start = ((), (), s32[]{:S(2)}) async-start(), calls=%async_computation.2 | async-start | bytes 8421376 | tf_op jit(solution)/shard_map/all_gather | solution.py:61
  7.9 2145.4 %reduce-scatter.2.cloned.1.call-start = ((), (), s32[]{:S(2)}) async-start(), calls=%async_computation.1 | async-start | bytes 16842752 | tf_op jit(solution)/shard_map/reduce_scatter | solution.py:75
  742.4 1.9 copy-start.1
  742.4 1.9 copy-start.3
  744.0 2.1 copy-start.5
  744.3 1.8 copy-start.2
  746.1 1.5 copy-start.4
  761.2 1.9 copy-start.1
  761.2 1.9 copy-start.3
  762.8 2.1 copy-start.5
  763.2 1.8 copy-start.2
  764.9 1.5 copy-start.4
  780.1 1.9 copy-start.1
  780.1 1.9 copy-start.3
  781.7 2.1 copy-start.5
  782.0 1.8 copy-start.2
  783.8 1.5 copy-start.4
  799.0 1.9 copy-start.1
  799.0 1.9 copy-start.3
  800.6 2.1 copy-start.5
  801.0 1.8 copy-start.2
  802.7 1.5 copy-start.4
Sparse Core Ops, SparseCore 0:
  9.9 709.3 all-gather.2
  854.9 1298.4 reduce-scatter.1
where the time goes:
time: 2170 us; the launch traced here: 2160 us
  waiting for transfers between devices  2000 us (92%)
  matrix products  75.7 us (3%)
  local copies, waits for them, and re-layouts  67.2 us (3%)
    reduce_scatter x1, waiting for transfers between devices, on_device(): lax.psum_scatter(arranged, ('dp', 'pipe'), scatter_dimension=0, tiled=True)  1290 us
    all_gather x1, waiting for transfers between devices, on_device(): lax.all_gather(kv_weight[None], ('dp', 'pipe'), axis=0, tiled=True)  702 us
  transfers between devices with their start and end apart: 2, of which 2 were waited for; matrix products, arithmetic and copies ran while one was open for 1% of the time, Pallas kernels for 0%

commit v1 on v0

v1 whole, which is shorter than its diff:
```python
import functools
import math

import jax
import jax.numpy as jnp
from jax import lax
from jax.experimental import pallas as pl
from jax.experimental.pallas import tpu as pltpu
from jax.sharding import PartitionSpec as P

SEQ = 384
WIDTH = 4096
HALF = 2048
KV_HEADS = 4
PAIRS = 4
HEAD = 128
SCALE = 1.0 / math.sqrt(HEAD)
LOG2E = math.log2(math.e)
MESH = pl.DeviceIdType.MESH
F32 = jnp.float32
BF16 = jnp.bfloat16
NT = (((1,), (1,)), ((), ()))


def place(x, y, z, c):
    return (z * 4 + (x // 2) * 2 + c, y * 2 + x % 2)


def kernel(
    tokens, queries, weight, cotangent, attended, kv_grad,
    tok, qry, cot, out, gathered, head_weight, part_send, part_own, part_recv,
    kv, d_kv, d_kv_t, acc, u_half, u_full, v_half, v_full, z_recv, done, owned,
    load_sem, tok_sem, ag_send, ag_recv, part_ssem, part_rsem, dkv_ssem, dkv_rsem,
    u_ssem, u_rsem, v_ssem, v_rsem, z_ssem, z_rsem, own_ssem, own_rsem, out_sem,
):
    dp, pipe = lax.axis_index("dp"), lax.axis_index("pipe")
    c, x, y, z = dp % 2, 2 * ((dp // 2) % 2) + pipe % 2, pipe // 2, dp // 4
    u, v = x + c * (y - x), y + c * (x - y)

    def uv(a, b):
        return place(a + c * (b - a), b + c * (a - b), z, c)

    def u_dev(step):
        return uv((u + step) % 4, v)

    def v_dev(step):
        return uv(u, (v + step) % 4)

    def z_dev(step):
        return place(x, y, (z + step) % 8, c)

    sibling = place(x, y, z, 1 - c)
    quad = 2 * (y % 2) + x % 2

    def remote(src, dst, ssem, rsem, device):
        return pltpu.make_async_remote_copy(
            src_ref=src, dst_ref=dst, send_sem=ssem, recv_sem=rsem,
            device_id=device, device_id_type=MESH,
        )

    own_weight = pltpu.make_async_copy(weight, gathered.at[u, v, z], load_sem.at[0])
    own_weight.start()

    def load_tokens(k, _):
        pltpu.make_async_copy(
            tokens.at[:, pl.ds(pl.multiple_of((2 * k + c) * 128, 128), 128)],
            tok.at[pl.ds(pl.multiple_of(c * SEQ, SEQ), SEQ), pl.ds(pl.multiple_of(k * 128, 128), 128)],
            load_sem.at[1],
        ).start()
        return 0

    lax.fori_loop(0, 16, load_tokens, 0)
    all_queries = pltpu.make_async_copy(queries, qry, load_sem.at[2])
    all_cot = pltpu.make_async_copy(cotangent, cot, load_sem.at[3])
    all_queries.start()
    all_cot.start()

    barrier = pltpu.get_barrier_semaphore()
    peers = [u_dev(1), u_dev(-1 + 4), v_dev(1), v_dev(-1 + 4), sibling]
    peers += [z_dev(k) for k in range(1, 8)]
    peers += [place(x + 1 - 2 * (x % 2), y + 1 - 2 * (y % 2), z, c)]
    for peer in peers:
        pl.semaphore_signal(barrier, inc=1, device_id=peer, device_id_type=MESH)
    pl.semaphore_wait(barrier, len(peers))

    own_weight.wait()
    mine = gathered.at[u, v, z]
    for k in range(1, 8):
        remote(mine, mine, ag_send.at[k], ag_recv.at[k], z_dev(k)).start()

    my_rows = pl.ds(pl.multiple_of(c * SEQ, SEQ), SEQ)
    sib_rows = pl.ds(pl.multiple_of((1 - c) * SEQ, SEQ), SEQ)

    def send_tokens(k, _):
        remote(
            tokens.at[:, pl.ds(pl.multiple_of((2 * k + 1 - c) * 128, 128), 128)],
            tok.at[my_rows, pl.ds(pl.multiple_of(k * 128, 128), 128)],
            tok_sem.at[0], tok_sem.at[1], sibling,
        ).start()
        return 0

    lax.fori_loop(0, 16, send_tokens, 0)

    for k in range(1, 8):
        here = gathered.at[u, v, (z - k + 8) % 8]
        remote(mine, here, ag_send.at[k], ag_recv.at[k], z_dev(k)).wait_recv()

    def v_first(step, sem):
        row = gathered.at[u, v]
        return remote(row, row, ag_send.at[sem], ag_recv.at[sem], v_dev(step))

    def v_second(step, sem):
        row = gathered.at[u, (v - step + 4) % 4, pl.ds(0 if step == 1 else 4, 4)]
        return remote(row, row, ag_send.at[sem], ag_recv.at[sem], v_dev((step + 4) % 4))

    def u_first(step, rel, sem):
        row = gathered.at[u, (v + rel + 4) % 4]
        return remote(row, row, ag_send.at[sem], ag_recv.at[sem], u_dev((step + 4) % 4))

    def u_second(step, rel, sem):
        row = gathered.at[(u - step + 4) % 4, (v + rel + 4) % 4, pl.ds(0 if step == 1 else 4, 4)]
        return remote(row, row, ag_send.at[sem], ag_recv.at[sem], u_dev((step + 4) % 4))

    rels = (0, -1, 1, 2)
    va = [v_first(1, 8), v_first(3, 9)]
    vb = [v_second(1, 10), v_second(-1, 11)]
    ua = {r: [u_first(1, r, 12 + 2 * i), u_first(-1, r, 13 + 2 * i)] for i, r in enumerate(rels)}
    ub = {r: [u_second(1, r, 20 + 2 * i), u_second(-1, r, 21 + 2 * i)] for i, r in enumerate(rels)}

    def start(copies):
        for copy in copies:
            copy.start()

    def landed(copies):
        for copy in copies:
            copy.wait_recv()

    def sent(copies):
        for copy in copies:
            copy.wait_send()

    start(va)
    start(ua[0])
    landed(va)
    start(vb)
    start(ua[-1])
    start(ua[1])
    landed(ua[0])
    start(ub[0])
    landed(vb)
    start(ua[2])
    landed(ua[-1])
    start(ub[-1])
    landed(ua[1])
    start(ub[1])
    landed(ua[2])
    start(ub[2])
    own_tok = pltpu.make_async_copy(tok.at[my_rows], tok.at[my_rows], load_sem.at[1])
    own_tok.wait()
    tok_all = remote(tok.at[my_rows], tok.at[sib_rows], tok_sem.at[0], tok_sem.at[1], sibling)
    tok_all.wait_recv()
    for r in rels:
        landed(ub[r])

    def part_copy(n):
        return remote(part_send.at[n], part_recv.at[n], part_ssem.at[n], part_rsem.at[n], sibling)

    def project(n):
        for kind in range(2):
            for x_hi in range(2):
                wx, wy = 2 * x_hi + n % 2, n // 2 + 2 * kind
                wu, wv = wx + c * (wy - wx), wy + c * (wx - wy)
                for wz in range(8):
                    k = wz * 2 + x_hi
                    head_weight[kind * 128:(kind + 1) * 128, k * 128:(k + 1) * 128] = gathered[wu, wv, wz]
        part_send[n] = lax.dot_general(tok[sib_rows, :], head_weight[...], NT, preferred_element_type=F32)
        part_copy(n).start()
        part_own[n] = lax.dot_general(tok[my_rows, :], head_weight[...], NT, preferred_element_type=F32)

    def attend(n, p):
        base = pl.multiple_of((n * PAIRS + p) * 256, 256)
        for j in range(3):
            rows, span = slice(j * 128, (j + 1) * 128), (j + 1) * 128
            q = qry[rows, pl.ds(base, 256)]
            g = cot[rows, pl.ds(base, 256)]
            q = jnp.concatenate([q[:, :128], q[:, 128:]], axis=0)
            g = jnp.concatenate([g[:, :128], g[:, 128:]], axis=0)
            keys, values = kv[:span, :128], kv[:span, 128:]
            scores = lax.dot_general(keys, q, NT, preferred_element_type=F32) * SCALE
            at_key = lax.broadcasted_iota(jnp.int32, (128, 256), 0)
            at_query = lax.broadcasted_iota(jnp.int32, (128, 256), 1) % 128
            diagonal = jnp.where(at_key <= at_query, scores[j * 128:], -1e30)
            scores = diagonal if j == 0 else jnp.concatenate([scores[: j * 128], diagonal], axis=0)
            top = jnp.max(scores, axis=0, keepdims=True)
            grown = jnp.exp2((scores - top) * LOG2E)
            probs = grown * (1.0 / jnp.sum(grown, axis=0, keepdims=True))
            probs_half = probs.astype(BF16)
            seen = lax.dot_general(
                values, probs_half, (((0,), (0,)), ((), ())), preferred_element_type=F32
            ).astype(BF16)
            out[rows, pl.ds(base, 128)] = seen[:, :128].T
            out[rows, pl.ds(base + 128, 128)] = seen[:, 128:].T
            d_probs = lax.dot_general(values, g, NT, preferred_element_type=F32)
            inner = jnp.sum(probs * d_probs, axis=0, keepdims=True)
            d_scores = (probs * (d_probs - inner) * SCALE).astype(BF16)
            d_kv[:span, :128] += jnp.dot(d_scores, q, preferred_element_type=F32)
            d_kv[:span, 128:] += jnp.dot(probs_half, g, preferred_element_type=F32)

    def dkv_copy(n):
        here = d_kv_t.at[n, :, my_rows]
        return remote(here, here, dkv_ssem.at[n], dkv_rsem.at[n], sibling)

    def dkv_landed(n):
        here = d_kv_t.at[n, :, sib_rows]
        remote(here, here, dkv_ssem.at[n], dkv_rsem.at[n], sibling).wait_recv()

    def gradient(n):
        lhs = d_kv_t[n]

        @pl.loop(0, 8)
        def _(gz):
            cols = pl.ds(pl.multiple_of(gz * 256, 256), 256)
            block = jnp.dot(lhs, tok[:, cols], preferred_element_type=F32)
            for kind in range(2):
                for q in range(4):
                    for x_hi in range(2):
                        gx, gy = 2 * x_hi + q % 2, 2 * kind + q // 2
                        gu, gv = gx + c * (gy - gx), gy + c * (gx - gy)
                        row = kind * 128 + q * 32
                        acc[n, gu, gv, gz] = block[row:row + 32, x_hi * 128:(x_hi + 1) * 128]

    def u_halves(n):
        far = (u + 2) % 4
        return [
            remote(acc.at[n, far, :, pl.ds(4 * i, 4)], u_half.at[n, i], u_ssem.at[n, i], u_rsem.at[n, i], u_dev(1 + 2 * i))
            for i in range(2)
        ]

    def u_fulls(n):
        return [
            remote(acc.at[n, (u + 1 + 2 * i) % 4], u_full.at[n, i], u_ssem.at[n, 2 + i], u_rsem.at[n, 2 + i], u_dev(1 + 2 * i))
            for i in range(2)
        ]

    def v_halves(n):
        far = (v + 2) % 4
        return [
            remote(acc.at[n, u, far, pl.ds(4 * i, 4)], v_half.at[n, i], v_ssem.at[n, i], v_rsem.at[n, i], v_dev(1 + 2 * i))
            for i in range(2)
        ]

    def v_fulls(n):
        return [
            remote(acc.at[n, u, (v + 1 + 2 * i) % 4], v_full.at[n, i], v_ssem.at[n, 2 + i], v_rsem.at[n, 2 + i], v_dev(1 + 2 * i))
            for i in range(2)
        ]

    def z_all(n):
        return [
            remote(acc.at[n, u, v, (z + k) % 8], z_recv.at[n, k - 1], z_ssem.at[n, k - 1], z_rsem.at[n, k - 1], z_dev(k))
            for k in range(1, 8)
        ]

    def to_owner(n):
        there = place(x - x % 2 + n % 2, y - y % 2 + n // 2, z, c)
        return remote(done.at[n], owned.at[quad], own_ssem.at[n], own_rsem.at[quad], there)

    def stage0(n):
        start(u_halves(n))

    def stage1(n):
        copies = u_halves(n)
        landed(copies)
        for i in range(2):
            near = (u + 1 + 2 * i) % 4
            for b in range(4):
                acc[n, near, b, pl.ds(4 * i, 4)] += u_half[n, i, b]
        start(u_fulls(n))
        sent(copies)

    def stage2(n):
        copies = u_fulls(n)
        landed(copies)
        for b in range(4):
            acc[n, u, b] += u_full[n, 0, b] + u_full[n, 1, b]
        start(v_halves(n))
        sent(copies)

    def stage3(n):
        copies = v_halves(n)
        landed(copies)
        for i in range(2):
            near = (v + 1 + 2 * i) % 4
            acc[n, u, near, pl.ds(4 * i, 4)] += v_half[n, i]
        start(v_fulls(n))
        sent(copies)

    def stage4(n):
        copies = v_fulls(n)
        landed(copies)
        acc[n, u, v] += v_full[n, 0] + v_full[n, 1]
        start(z_all(n))
        sent(copies)

    def stage5(n):
        copies = z_all(n)
        landed(copies)
        total = acc[n, u, v, z]
        for k in range(7):
            total = total + z_recv[n, k]

        @pl.when(quad == n)
        def _():
            owned[quad] = total

        @pl.when(quad != n)
        def _():
            done[n] = total
            to_owner(n).start()

        sent(copies)

    def out_copy(n):
        cols = pl.ds(pl.multiple_of(n * 1024, 1024), 1024)
        return pltpu.make_async_copy(out.at[:, cols], attended.at[:, cols], out_sem.at[n])

    project(0)
    project(1)
    project(2)
    project(3)
    all_queries.wait()
    all_cot.wait()

    def head(n, _):
        part_copy(n).wait_recv()
        kv[...] = (part_own[n] + part_recv[n]).astype(BF16)
        d_kv[...] = jnp.zeros_like(d_kv)
        attend(n, 0)
        pl.when(n >= 2)(lambda: stage3(n - 2))
        attend(n, 1)
        pl.when(n >= 1)(lambda: stage1(n - 1))
        attend(n, 2)
        pl.when(n >= 2)(lambda: stage4(n - 2))
        attend(n, 3)
        out_copy(n).start()
        d_kv_t[n, :, my_rows] = d_kv[...].astype(BF16).T
        dkv_copy(n).start()
        dkv_landed(n)
        gradient(n)
        stage0(n)
        pl.when(n >= 1)(lambda: stage2(n - 1))
        pl.when(n >= 2)(lambda: stage5(n - 2))
        return 0

    lax.fori_loop(0, KV_HEADS, head, 0)
    stage3(2)
    stage1(3)
    stage4(2)
    stage2(3)
    stage5(2)
    stage3(3)
    stage4(3)
    stage5(3)

    for q in range(4):

        @pl.when(quad != q)
        def _():
            to_owner(q).wait_send()
            remote(done.at[q], owned.at[q], own_ssem.at[q], own_rsem.at[q], sibling).wait_recv()

    for q in range(4):
        kv_grad[q * 32:(q + 1) * 32, :] = owned[q]
    for k in range(1, 8):
        remote(mine, mine, ag_send.at[k], ag_recv.at[k], z_dev(k)).wait_send()
    sent(va)
    sent(vb)
    for r in rels:
        sent(ua[r])
        sent(ub[r])
    tok_all.wait_send()
    for n in range(KV_HEADS):
        part_copy(n).wait_send()
        dkv_copy(n).wait_send()
        out_copy(n).wait()


def on_device(tokens, queries, weight, cotangent):
    anywhere = pl.BlockSpec(memory_space=pl.ANY)
    vmem = pltpu.VMEM
    dma = pltpu.SemaphoreType.DMA
    return pl.pallas_call(
        kernel,
        out_shape=(
            jax.ShapeDtypeStruct((SEQ, WIDTH), BF16),
            jax.ShapeDtypeStruct((128, 128), F32),
        ),
        in_specs=[anywhere] * 4,
        out_specs=(anywhere, pl.BlockSpec(memory_space=vmem)),
        scratch_shapes=[
            vmem((2 * SEQ, HALF), BF16),
            vmem((SEQ, WIDTH), BF16),
            vmem((SEQ, WIDTH), BF16),
            vmem((SEQ, WIDTH), BF16),
            vmem((4, 4, 8, 128, 128), BF16),
            vmem((256, HALF), BF16),
            vmem((4, SEQ, 256), F32),
            vmem((4, SEQ, 256), F32),
            vmem((4, SEQ, 256), F32),
            vmem((SEQ, 256), BF16),
            vmem((SEQ, 256), F32),
            vmem((4, 256, 2 * SEQ), BF16),
            vmem((4, 4, 4, 8, 32, 128), F32),
            vmem((4, 2, 4, 4, 32, 128), F32),
            vmem((4, 2, 4, 8, 32, 128), F32),
            vmem((4, 2, 4, 32, 128), F32),
            vmem((4, 2, 8, 32, 128), F32),
            vmem((4, 7, 32, 128), F32),
            vmem((4, 32, 128), F32),
            vmem((4, 32, 128), F32),
            dma((4,)),
            dma((2,)),
            dma((28,)),
            dma((28,)),
            dma((4,)),
            dma((4,)),
            dma((4,)),
            dma((4,)),
            dma((4, 4)),
            dma((4, 4)),
            dma((4, 4)),
            dma((4, 4)),
            dma((4, 7)),
            dma((4, 7)),
            dma((4,)),
            dma((4,)),
            dma((4,)),
        ],
        compiler_params=pltpu.CompilerParams(
            collective_id=0, has_side_effects=True, vmem_limit_bytes=56 * 2**20
        ),
        cost_estimate=pl.CostEstimate(flops=12 * 10**9, bytes_accessed=16 * 2**20, transcendentals=4 * 10**6),
    )(tokens, queries, weight, cotangent)


def solution(mesh):
    placed = (
        P(("dp", "pipe"), None),
        P(("dp", "pipe"), None),
        P("pipe", "dp"),
        P(("dp", "pipe"), None),
    )
    return jax.shard_map(
        on_device,
        mesh=mesh,
        in_specs=placed,
        out_specs=(P(("dp", "pipe"), None), P("pipe", "dp")),
        check_vma=False,
    )
```

time: 2170 us -> 142 us (0.07)
  waiting for transfers between devices: 2000 us -> 0 us
  Pallas kernels: 0 us -> 137 us
  matrix products: 75.7 us -> 0 us
  local copies, waits for them, and re-layouts: 67.2 us -> 4.57 us
    reduce_scatter x1 -> x0, waiting for transfers between devices: 1290 us -> none  [on_device(): lax.psum_scatter(arranged, ('dp', 'pipe'), scatter_dimension=0, tiled=True)]
    all_gather x1 -> x0, waiting for transfers between devices: 702 us -> none  [on_device(): lax.all_gather(kv_weight[None], ('dp', 'pipe'), axis=0, tiled=True)]
    pallas_call x0 -> x1, Pallas kernels: none -> 137 us  [on_device(): pl.pallas_call(kernel, out_shape=(jax.ShapeDtypeStruct((SEQ, WIDTH), BF16...]
    dot_general x22 -> x0, matrix products: 75.7 us -> none  [the longest x4 35 us: group_pass(): jnp.einsum('gst,sgd->td', d_scores, query_group, preferred_element_type=j...]
    transpose x2 -> x0, local copies, waits for them, and re-layouts: 26.3 us -> none  [on_device(): arranged.transpose(2, 0, 1, 3)]
  transfers between devices with their start and end apart: 2 -> 0, of which waited for: 2 -> 0; matrix products, arithmetic and copies ran while one was open for 1% -> 0% of each run, Pallas kernels for 0% -> 0%
where the time goes in v1:
time: 142 us
  Pallas kernels  137 us (96%)
  local copies, waits for them, and re-layouts  4.57 us (3%)
    pallas_call x1, Pallas kernels, on_device(): pl.pallas_call(kernel, out_shape=(jax.ShapeDtypeStruct((SEQ, WIDTH), BF16...  137 us
    unnamed x4, local copies, waits for them, and re-layouts  4.57 us

profile of v1, /device:TPU:10, one launch (start us, length us, event | category | flops | bytes accessed | tf_op | source)
XLA Modules:
  0.0 141.8 jit_solution(338658727188178231)
XLA Ops:
  0.6 136.5 %shard_map.59 = (bf16[384,4096]{1,0:T(8,128)(2,1)}, f32[128,128]{1,0:T(8,128)}) custom-call(bf16[384,4096]{1,0:T(8,128)(2,1)} %tokens.1, bf16[384,4096]{1,0:T(8,128)(2,1)} %queries.1, bf16[128,128]{1,0:T(8,128)(2,1)} %weight.1, bf16[384,4096]{1,0:T(8,128)(2,1)} %cotangent.1), custom_call_target="tpu_custom_call" | custom-call | flops 12000000000 | bytes 16777216 | tf_op jit(solution)/shard_map/pallas_call | solution.py:392
  137.2 0.0 copy-start
  137.2 3.9 %copy.8 = bf16[384,4096]{1,0:T(8,128)(2,1)} copy(bf16[384,4096]{1,0:T(8,128)(2,1)} %get-tuple-element.4) | data formatting | bytes 6291456
  141.1 0.0 copy-done
  141.1 0.6 copy.9
Async XLA Ops:
  137.2 4.0 %copy-start = (f32[128,128]{1,0:T(8,128)S(1)}, f32[128,128]{1,0:T(8,128)}, u32[]{:S(2)}) copy-start(f32[128,128]{1,0:T(8,128)} %get-tuple-element.5) | copy-start | bytes 196612

commit v2 on v1

v2 whole, which is shorter than its diff:
```python
import functools
import math

import jax
import jax.numpy as jnp
from jax import lax
from jax.experimental import pallas as pl
from jax.experimental.pallas import tpu as pltpu
from jax.sharding import PartitionSpec as P

SEQ = 384
WIDTH = 4096
HALF = 2048
KV_HEADS = 4
HEAD = 128
SCALE = 1.0 / math.sqrt(HEAD)
LOG2E = math.log2(math.e)
MESH = pl.DeviceIdType.MESH
F32 = jnp.float32
BF16 = jnp.bfloat16
MAIN = 96
NT = (((1,), (1,)), ((), ()))


def place(x, y, z, c):
    return (z * 4 + (x // 2) * 2 + c, y * 2 + x % 2)


def kernel(
    tokens, queries, weight, cotangent, attended, kv_grad,
    tok, far_tok, qry, cot, out, gathered, gathered_z, head_weight, part_send, part_own, part_recv,
    kv, d_kv, d_kv_t, far_kv_t, acc, u_half, u_full, v_recv, z_recv, done, owned,
    load_sem, tok_sem, ag_send, ag_recv, zg_send, zg_recv, part_ssem, part_rsem, dkv_ssem, dkv_rsem, far_send, far_recv,
    u_ssem, u_rsem, v_ssem, v_rsem, z_ssem, z_rsem, own_ssem, own_rsem, out_sem,
):
    dp, pipe = lax.axis_index("dp"), lax.axis_index("pipe")
    c, x, y, z = dp % 2, 2 * ((dp // 2) % 2) + pipe % 2, pipe // 2, dp // 4
    u, v = x + c * (y - x), y + c * (x - y)

    def uv(a, b):
        return place(a + c * (b - a), b + c * (a - b), z, c)

    def u_dev(step):
        return uv((u + step) % 4, v)

    def v_dev(step):
        return uv(u, (v + step) % 4)

    def z_dev(step):
        return place(x, y, (z + step) % 8, c)

    sibling = place(x, y, z, 1 - c)
    z_odd, z_half = z % 2, z // 2
    partner = [place(x, y, z + 1 - 2 * z_odd, c), place(x, y, z + 1 - 2 * z_odd, 1 - c)]
    quad = 2 * (y % 2) + x % 2

    def remote(src, dst, ssem, rsem, device):
        return pltpu.make_async_remote_copy(
            src_ref=src, dst_ref=dst, send_sem=ssem, recv_sem=rsem,
            device_id=device, device_id_type=MESH,
        )

    own_weight = pltpu.make_async_copy(weight.at[pl.ds(0, MAIN)], gathered.at[u, v, z], load_sem.at[0])
    own_rest = pltpu.make_async_copy(weight.at[pl.ds(MAIN, 128 - MAIN)], gathered_z.at[z, u, v], load_sem.at[4])
    own_weight.start()
    own_rest.start()

    def load_tokens(k, _):
        pltpu.make_async_copy(
            tokens.at[:, pl.ds(pl.multiple_of((2 * k + c) * 128, 128), 128)],
            tok.at[pl.ds(pl.multiple_of(c * SEQ, SEQ), SEQ), pl.ds(pl.multiple_of(k * 128, 128), 128)],
            load_sem.at[1],
        ).start()
        return 0

    lax.fori_loop(0, 16, load_tokens, 0)
    all_queries = pltpu.make_async_copy(queries, qry, load_sem.at[2])
    all_cot = pltpu.make_async_copy(cotangent, cot, load_sem.at[3])
    all_queries.start()
    all_cot.start()

    barrier = pltpu.get_barrier_semaphore()
    peers = [u_dev(k) for k in range(1, 4)] + [v_dev(k) for k in range(1, 4)] + [sibling]
    peers += [z_dev(k) for k in range(1, 8)]
    peers += [place(x + 1 - 2 * (x % 2), y + 1 - 2 * (y % 2), z, c), partner[1]]
    for peer in peers:
        pl.semaphore_signal(barrier, inc=1, device_id=peer, device_id_type=MESH)
    pl.semaphore_wait(barrier, len(peers))

    own_weight.wait()
    mine = gathered.at[u, v, z]
    for k in range(1, 8):
        remote(mine, mine, ag_send.at[k], ag_recv.at[k], z_dev(k)).start()

    own_rest.wait()

    def zv(k):
        here = gathered_z.at[z, u, v]
        return remote(here, here, zg_send.at[k], zg_recv.at[k], v_dev(k))

    def zu(k):
        here = gathered_z.at[z, u]
        return remote(here, here, zg_send.at[3 + k], zg_recv.at[3 + k], u_dev(k))

    def zz(hop, way):
        here = gathered_z.at[(z - way * hop + 8) % 8]
        if hop == 3:
            here = here.at[pl.ds(0 if way == 1 else 2, 2)]
        sem = 7 + 2 * hop + (way == -1)
        return remote(here, here, zg_send.at[sem], zg_recv.at[sem], z_dev(8 + way))

    zvs = [zv(k) for k in range(1, 4)]
    zus = [zu(k) for k in range(1, 4)]
    zzs = [[zz(hop, 1), zz(hop, -1)] for hop in range(4)]
    for copy in zvs:
        copy.start()

    my_rows = pl.ds(pl.multiple_of(c * SEQ, SEQ), SEQ)
    sib_rows = pl.ds(pl.multiple_of((1 - c) * SEQ, SEQ), SEQ)

    def send_tokens(k, _):
        remote(
            tokens.at[:, pl.ds(pl.multiple_of((2 * k + 1 - c) * 128, 128), 128)],
            tok.at[my_rows, pl.ds(pl.multiple_of(k * 128, 128), 128)],
            tok_sem.at[0], tok_sem.at[1], sibling,
        ).start()
        return 0

    lax.fori_loop(0, 16, send_tokens, 0)

    def v_first(step, sem):
        row = gathered.at[u, v]
        return remote(row, row, ag_send.at[sem], ag_recv.at[sem], v_dev(step))

    def v_second(step, sem):
        row = gathered.at[u, (v - step + 4) % 4, pl.ds(0 if step == 1 else 4, 4)]
        return remote(row, row, ag_send.at[sem], ag_recv.at[sem], v_dev((step + 4) % 4))

    def u_first(step, rel, sem):
        row = gathered.at[u, (v + rel + 4) % 4]
        return remote(row, row, ag_send.at[sem], ag_recv.at[sem], u_dev((step + 4) % 4))

    def u_second(step, rel, sem):
        row = gathered.at[(u - step + 4) % 4, (v + rel + 4) % 4, pl.ds(0 if step == 1 else 4, 4)]
        return remote(row, row, ag_send.at[sem], ag_recv.at[sem], u_dev((step + 4) % 4))

    rels = (0, -1, 1, 2)
    va = [v_first(1, 8), v_first(3, 9)]
    vb = [v_second(1, 10), v_second(-1, 11)]
    ua = {r: [u_first(1, r, 12 + 2 * i), u_first(-1, r, 13 + 2 * i)] for i, r in enumerate(rels)}
    ub = {r: [u_second(1, r, 20 + 2 * i), u_second(-1, r, 21 + 2 * i)] for i, r in enumerate(rels)}

    def start(copies):
        for copy in copies:
            copy.start()

    def landed(copies):
        for copy in copies:
            copy.wait_recv()

    def sent(copies):
        for copy in copies:
            copy.wait_send()

    def share(first, last):
        for i in range(first, last):
            core, block = i // 8, i % 8
            target = c if core == 0 else 1 - c
            column = (2 * (block // 2) + 1 - z_odd) * 4 + 2 * (block % 2) + target
            remote(
                tokens.at[:, pl.ds(pl.multiple_of(column * 128, 128), 128)],
                far_tok.at[my_rows, pl.ds(block * 128, 128)],
                far_send.at[core], far_recv.at[core], partner[core],
            ).start()

    landed(zvs)
    start(zus)
    for k in range(1, 8):
        here = gathered.at[u, v, (z - k + 8) % 8]
        remote(mine, here, ag_send.at[k], ag_recv.at[k], z_dev(k)).wait_recv()
    start(va)
    start(ua[0])
    landed(zus)
    start(zzs[0])
    share(0, 2)
    landed(va)
    start(vb)
    start(ua[-1])
    start(ua[1])
    landed(zzs[0])
    start(zzs[1])
    share(2, 4)
    landed(ua[0])
    start(ub[0])
    landed(vb)
    start(ua[2])
    landed(zzs[1])
    start(zzs[2])
    share(4, 6)
    landed(ua[-1])
    start(ub[-1])
    landed(ua[1])
    start(ub[1])
    landed(zzs[2])
    start(zzs[3])
    share(6, 16)
    landed(ua[2])
    start(ub[2])
    own_tok = pltpu.make_async_copy(tok.at[my_rows], tok.at[my_rows], load_sem.at[1])
    own_tok.wait()
    tok_all = remote(tok.at[my_rows], tok.at[sib_rows], tok_sem.at[0], tok_sem.at[1], sibling)
    tok_all.wait_recv()
    for r in rels:
        landed(ub[r])
    landed(zzs[3])

    def part_copy(n):
        return remote(part_send.at[n], part_recv.at[n], part_ssem.at[n], part_rsem.at[n], sibling)

    def project(n):
        for kind in range(2):
            for x_hi in range(2):
                wx, wy = 2 * x_hi + n % 2, n // 2 + 2 * kind
                wu, wv = wx + c * (wy - wx), wy + c * (wx - wy)
                for wz in range(8):
                    k = wz * 2 + x_hi
                    cols, row = slice(k * 128, (k + 1) * 128), kind * 128
                    head_weight[row:row + MAIN, cols] = gathered[wu, wv, wz]
                    head_weight[row + MAIN:row + 128, cols] = gathered_z[wz, wu, wv]
        part_send[n] = lax.dot_general(tok[sib_rows, :], head_weight[...], NT, preferred_element_type=F32)
        part_copy(n).start()
        part_own[n] = lax.dot_general(tok[my_rows, :], head_weight[...], NT, preferred_element_type=F32)

    def attend(n, p):
        base = pl.multiple_of((n * 2 + p) * 512, 512)
        at_key = lax.broadcasted_iota(jnp.int32, (128, 512), 0)
        at_query = lax.broadcasted_iota(jnp.int32, (128, 512), 1) % 128

        def heads(ref, j):
            block = ref[j * 128:(j + 1) * 128, pl.ds(base, 512)]
            return jnp.concatenate([block[:, h * 128:(h + 1) * 128] for h in range(4)], axis=0)

        def products(j):
            q, g, span = heads(qry, j), heads(cot, j), (j + 1) * 128
            scores = lax.dot_general(kv[:span, :128], q, NT, preferred_element_type=F32)
            d_probs = lax.dot_general(kv[:span, 128:], g, NT, preferred_element_type=F32)
            return q, g, scores, d_probs

        def softmax(j, scores, d_probs):
            diagonal = jnp.where(at_key <= at_query, scores[j * 128:], -1e30)
            scores = diagonal if j == 0 else jnp.concatenate([scores[: j * 128], diagonal], axis=0)
            top = jnp.max(scores, axis=0, keepdims=True)
            grown = jnp.exp2((scores - top) * (SCALE * LOG2E))
            share_of = 1.0 / jnp.sum(grown, axis=0, keepdims=True)
            weighed = grown * d_probs
            inner = jnp.sum(weighed, axis=0, keepdims=True) * share_of
            d_scores = (weighed - grown * inner) * (share_of * SCALE)
            return (grown * share_of).astype(BF16), d_scores.astype(BF16)

        blocks = [products(j) for j in range(3)]
        halves = [softmax(j, blocks[j][2], blocks[j][3]) for j in range(3)]
        d_keys, d_values = [], []
        for j in range(3):
            q, g = blocks[j][:2]
            probs_half, d_scores = halves[j]
            seen = lax.dot_general(
                kv[: (j + 1) * 128, 128:], probs_half, (((0,), (0,)), ((), ())), preferred_element_type=F32
            ).astype(BF16)
            for h in range(4):
                out[j * 128:(j + 1) * 128, pl.ds(base + h * 128, 128)] = seen[:, h * 128:(h + 1) * 128].T
            d_keys.append(jnp.dot(d_scores, q, preferred_element_type=F32))
            d_values.append(jnp.dot(probs_half, g, preferred_element_type=F32))
        for t in range(3):
            rows = slice(t * 128, (t + 1) * 128)
            d_kv[rows, :128] += sum(d_keys[j][rows] for j in range(t, 3))
            d_kv[rows, 128:] += sum(d_values[j][rows] for j in range(t, 3))

    def dkv_copies(n):
        here, there = d_kv_t.at[n, :, my_rows], far_kv_t.at[n, :, my_rows]
        return [
            remote(here, here, dkv_ssem.at[n, 0], dkv_rsem.at[n, 0], sibling),
            remote(here, there, dkv_ssem.at[n, 1], dkv_rsem.at[n, 1], partner[0]),
            remote(there, there, dkv_ssem.at[n, 2], dkv_rsem.at[n, 2], sibling),
        ]

    def forward(n):
        copies = dkv_copies(n)
        copies[1].wait_recv()
        copies[2].start()

    def gradient(n):
        copies = dkv_copies(n)
        copies[0].wait_recv()
        if n == 0:
            for core in range(2):
                rows = far_tok.at[my_rows if core == 0 else sib_rows]
                remote(rows, rows, far_send.at[core], far_recv.at[core], partner[core]).wait_recv()
        copies[2].wait_recv()
        near, far = d_kv_t[n], far_kv_t[n]

        @pl.loop(0, 4)
        def _(gz):
            cols = pl.ds(pl.multiple_of((2 * gz + z_odd) * 256, 256), 256)
            far_cols = pl.ds(pl.multiple_of(gz * 256, 256), 256)
            block = jnp.dot(near, tok[:, cols], preferred_element_type=F32)
            block += jnp.dot(far, far_tok[:, far_cols], preferred_element_type=F32)
            for kind in range(2):
                for q in range(4):
                    for x_hi in range(2):
                        gx, gy = 2 * x_hi + q % 2, 2 * kind + q // 2
                        gu, gv = gx + c * (gy - gx), gy + c * (gx - gy)
                        row = kind * 128 + q * 32
                        acc[n, gu, gv, gz] = block[row:row + 32, x_hi * 128:(x_hi + 1) * 128]

    def u_halves(n):
        far = (u + 2) % 4
        return [
            remote(acc.at[n, far, :, pl.ds(2 * i, 2)], u_half.at[n, i], u_ssem.at[n, i], u_rsem.at[n, i], u_dev(1 + 2 * i))
            for i in range(2)
        ]

    def u_fulls(n):
        return [
            remote(acc.at[n, (u + 1 + 2 * i) % 4], u_full.at[n, i], u_ssem.at[n, 2 + i], u_rsem.at[n, 2 + i], u_dev(1 + 2 * i))
            for i in range(2)
        ]

    def v_all(n):
        return [
            remote(acc.at[n, u, (v + k) % 4], v_recv.at[n, k - 1], v_ssem.at[n, k - 1], v_rsem.at[n, k - 1], v_dev(k))
            for k in range(1, 4)
        ]

    def z_all(n):
        return [
            remote(acc.at[n, u, v, (z_half + k) % 4], z_recv.at[n, k - 1], z_ssem.at[n, k - 1], z_rsem.at[n, k - 1], z_dev(2 * k))
            for k in range(1, 4)
        ]

    def to_owner(n):
        there = place(x - x % 2 + n % 2, y - y % 2 + n // 2, z, c)
        return remote(done.at[n], owned.at[quad], own_ssem.at[n], own_rsem.at[quad], there)

    def stage0(n):
        start(u_halves(n))

    def stage1(n):
        copies = u_halves(n)
        landed(copies)
        for i in range(2):
            near = (u + 1 + 2 * i) % 4
            for b in range(4):
                acc[n, near, b, pl.ds(2 * i, 2)] += u_half[n, i, b]
        start(u_fulls(n))
        sent(copies)

    def stage2(n):
        copies = u_fulls(n)
        landed(copies)
        for b in range(4):
            acc[n, u, b] += u_full[n, 0, b] + u_full[n, 1, b]
        start(v_all(n))
        sent(copies)

    def stage3(n):
        copies = v_all(n)
        landed(copies)
        acc[n, u, v] += (v_recv[n, 0] + v_recv[n, 1]) + v_recv[n, 2]
        start(z_all(n))
        sent(copies)

    def stage4(n):
        copies = z_all(n)
        landed(copies)
        total = (acc[n, u, v, z_half] + z_recv[n, 0]) + (z_recv[n, 1] + z_recv[n, 2])

        @pl.when(quad == n)
        def _():
            owned[quad] = total

        @pl.when(quad != n)
        def _():
            done[n] = total
            to_owner(n).start()

        sent(copies)

    def out_copy(n):
        cols = pl.ds(pl.multiple_of(n * 1024, 1024), 1024)
        return pltpu.make_async_copy(out.at[:, cols], attended.at[:, cols], out_sem.at[n])

    project(0)
    project(1)
    all_queries.wait()
    all_cot.wait()

    def head(n):
        part_copy(n).wait_recv()
        kv[...] = (part_own[n] + part_recv[n]).astype(BF16)
        d_kv[...] = jnp.zeros_like(d_kv)

        def half(p, _):
            attend(n, p)
            return 0

        lax.fori_loop(0, 2, half, 0)
        out_copy(n).start()
        d_kv_t[n, :, my_rows] = d_kv[...].astype(BF16).T
        start(dkv_copies(n)[:2])
        if n + 2 < KV_HEADS:
            project(n + 2)

    head(0)
    head(1)
    forward(0)
    gradient(0)
    stage0(0)
    head(2)
    forward(1)
    stage1(0)
    gradient(1)
    stage0(1)
    head(3)
    forward(2)
    stage1(1)
    stage2(0)
    gradient(2)
    stage0(2)
    forward(3)
    stage3(0)
    stage2(1)
    gradient(3)
    stage0(3)
    stage1(2)
    stage3(1)
    stage4(0)
    stage1(3)
    stage2(2)
    stage4(1)
    stage3(2)
    stage2(3)
    stage4(2)
    stage3(3)
    stage4(3)

    for q in range(4):

        @pl.when(quad != q)
        def _():
            to_owner(q).wait_send()
            remote(done.at[q], owned.at[q], own_ssem.at[q], own_rsem.at[q], sibling).wait_recv()

    for q in range(4):
        kv_grad[q * 32:(q + 1) * 32, :] = owned[q]
    for k in range(1, 8):
        remote(mine, mine, ag_send.at[k], ag_recv.at[k], z_dev(k)).wait_send()
    sent(va)
    sent(vb)
    for r in rels:
        sent(ua[r])
        sent(ub[r])
    sent(zvs)
    sent(zus)
    for copies in zzs:
        sent(copies)
    tok_all.wait_send()
    for core in range(2):
        rows = far_tok.at[my_rows]
        remote(rows, rows, far_send.at[core], far_recv.at[core], partner[core]).wait_send()
    for n in range(KV_HEADS):
        part_copy(n).wait_send()
        sent(dkv_copies(n))
        out_copy(n).wait()


def on_device(tokens, queries, weight, cotangent):
    anywhere = pl.BlockSpec(memory_space=pl.ANY)
    vmem = pltpu.VMEM
    dma = pltpu.SemaphoreType.DMA
    return pl.pallas_call(
        kernel,
        out_shape=(
            jax.ShapeDtypeStruct((SEQ, WIDTH), BF16),
            jax.ShapeDtypeStruct((128, 128), F32),
        ),
        in_specs=[anywhere] * 4,
        out_specs=(anywhere, pl.BlockSpec(memory_space=vmem)),
        scratch_shapes=[
            vmem((2 * SEQ, HALF), BF16),
            vmem((2 * SEQ, HALF // 2), BF16),
            vmem((SEQ, WIDTH), BF16),
            vmem((SEQ, WIDTH), BF16),
            vmem((SEQ, WIDTH), BF16),
            vmem((4, 4, 8, MAIN, 128), BF16),
            vmem((8, 4, 4, 128 - MAIN, 128), BF16),
            vmem((256, HALF), BF16),
            vmem((4, SEQ, 256), F32),
            vmem((4, SEQ, 256), F32),
            vmem((4, SEQ, 256), F32),
            vmem((SEQ, 256), BF16),
            vmem((SEQ, 256), F32),
            vmem((4, 256, 2 * SEQ), BF16),
            vmem((4, 256, 2 * SEQ), BF16),
            vmem((4, 4, 4, 4, 32, 128), F32),
            vmem((4, 2, 4, 2, 32, 128), F32),
            vmem((4, 2, 4, 4, 32, 128), F32),
            vmem((4, 3, 4, 32, 128), F32),
            vmem((4, 3, 32, 128), F32),
            vmem((4, 32, 128), F32),
            vmem((4, 32, 128), F32),
            dma((5,)),
            dma((2,)),
            dma((28,)),
            dma((28,)),
            dma((15,)),
            dma((15,)),
            dma((4,)),
            dma((4,)),
            dma((4, 3)),
            dma((4, 3)),
            dma((2,)),
            dma((2,)),
            dma((4, 4)),
            dma((4, 4)),
            dma((4, 3)),
            dma((4, 3)),
            dma((4, 3)),
            dma((4, 3)),
            dma((4,)),
            dma((4,)),
            dma((4,)),
        ],
        compiler_params=pltpu.CompilerParams(
            collective_id=0, has_side_effects=True, vmem_limit_bytes=56 * 2**20
        ),
        cost_estimate=pl.CostEstimate(flops=12 * 10**9, bytes_accessed=16 * 2**20, transcendentals=4 * 10**6),
    )(tokens, queries, weight, cotangent)


def solution(mesh):
    placed = (
        P(("dp", "pipe"), None),
        P(("dp", "pipe"), None),
        P("pipe", "dp"),
        P(("dp", "pipe"), None),
    )
    return jax.shard_map(
        on_device,
        mesh=mesh,
        in_specs=placed,
        out_specs=(P(("dp", "pipe"), None), P("pipe", "dp")),
        check_vma=False,
    )
```

time: 142 us -> 122 us (0.86)
  Pallas kernels: 137 us -> 116 us
    pallas_call x1, Pallas kernels: 137 us -> 116 us  [on_device(): pl.pallas_call(kernel, out_shape=(jax.ShapeDtypeStruct((SEQ, WIDTH), BF16...]
where the time goes in v2:
time: 122 us
  Pallas kernels  116 us (95%)
  local copies, waits for them, and re-layouts  4.57 us (4%)
    pallas_call x1, Pallas kernels, on_device(): pl.pallas_call(kernel, out_shape=(jax.ShapeDtypeStruct((SEQ, WIDTH), BF16...  116 us
    unnamed x4, local copies, waits for them, and re-layouts  4.57 us

profile of v2, /device:TPU:10, one launch (start us, length us, event | category | flops | bytes accessed | tf_op | source)
XLA Modules:
  0.0 121.6 jit_solution(9301959965908310752)
XLA Ops:
  0.6 116.4 %shard_map.59 = (bf16[384,4096]{1,0:T(8,128)(2,1)}, f32[128,128]{1,0:T(8,128)}) custom-call(bf16[384,4096]{1,0:T(8,128)(2,1)} %tokens.1, bf16[384,4096]{1,0:T(8,128)(2,1)} %queries.1, bf16[128,128]{1,0:T(8,128)(2,1)} %weight.1, bf16[384,4096]{1,0:T(8,128)(2,1)} %cotangent.1), custom_call_target="tpu_custom_call" | custom-call | flops 12000000000 | bytes 16777216 | tf_op jit(solution)/shard_map/pallas_call | solution.py:480
  117.0 0.0 copy-start
  117.0 3.9 %copy.8 = bf16[384,4096]{1,0:T(8,128)(2,1)} copy(bf16[384,4096]{1,0:T(8,128)(2,1)} %get-tuple-element.4) | data formatting | bytes 6291456
  121.0 0.0 copy-done
  121.0 0.6 copy.9
Async XLA Ops:
  117.0 4.0 %copy-start = (f32[128,128]{1,0:T(8,128)S(1)}, f32[128,128]{1,0:T(8,128)}, u32[]{:S(2)}) copy-start(f32[128,128]{1,0:T(8,128)} %get-tuple-element.5) | copy-start | bytes 196612

commit v3 on v2

--- a/solution.py
+++ b/solution.py
@@ -28,9 +28,9 @@
 
 def kernel(
     tokens, queries, weight, cotangent, attended, kv_grad,
-    tok, far_tok, qry, cot, out, gathered, gathered_z, head_weight, part_send, part_own, part_recv,
-    kv, d_kv, d_kv_t, far_kv_t, acc, u_half, u_full, v_recv, z_recv, done, owned,
-    load_sem, tok_sem, ag_send, ag_recv, zg_send, zg_recv, part_ssem, part_rsem, dkv_ssem, dkv_rsem, far_send, far_recv,
+    tok, tok_t, qry, cot, out, gathered, gathered_z, head_weight, part, part_recv,
+    kv, d_kv, d_kv_t, acc, u_half, u_full, v_half, v_full, z_recv, done, owned, zacc, z_half, z_full, zu_recv, zv_recv,
+    load_sem, tok_sem, ag_send, ag_recv, zg_send, zg_recv, part_ssem, part_rsem, dkv_ssem, dkv_rsem, zr_send, zr_recv,
     u_ssem, u_rsem, v_ssem, v_rsem, z_ssem, z_rsem, own_ssem, own_rsem, out_sem,
 ):
     dp, pipe = lax.axis_index("dp"), lax.axis_index("pipe")
@@ -50,8 +50,6 @@
         return place(x, y, (z + step) % 8, c)
 
     sibling = place(x, y, z, 1 - c)
-    z_odd, z_half = z % 2, z // 2
-    partner = [place(x, y, z + 1 - 2 * z_odd, c), place(x, y, z + 1 - 2 * z_odd, 1 - c)]
     quad = 2 * (y % 2) + x % 2
 
     def remote(src, dst, ssem, rsem, device):
@@ -82,7 +80,7 @@
     barrier = pltpu.get_barrier_semaphore()
     peers = [u_dev(k) for k in range(1, 4)] + [v_dev(k) for k in range(1, 4)] + [sibling]
     peers += [z_dev(k) for k in range(1, 8)]
-    peers += [place(x + 1 - 2 * (x % 2), y + 1 - 2 * (y % 2), z, c), partner[1]]
+    peers += [place(x + 1 - 2 * (x % 2), y + 1 - 2 * (y % 2), z, c)]
     for peer in peers:
         pl.semaphore_signal(barrier, inc=1, device_id=peer, device_id_type=MESH)
     pl.semaphore_wait(barrier, len(peers))
@@ -161,17 +159,6 @@
     def sent(copies):
         for copy in copies:
             copy.wait_send()
-
-    def share(first, last):
-        for i in range(first, last):
-            core, block = i // 8, i % 8
-            target = c if core == 0 else 1 - c
-            column = (2 * (block // 2) + 1 - z_odd) * 4 + 2 * (block % 2) + target
-            remote(
-                tokens.at[:, pl.ds(pl.multiple_of(column * 128, 128), 128)],
-                far_tok.at[my_rows, pl.ds(block * 128, 128)],
-                far_send.at[core], far_recv.at[core], partner[core],
-            ).start()
 
     landed(zvs)
     start(zus)
@@ -182,40 +169,48 @@
     start(ua[0])
     landed(zus)
     start(zzs[0])
-    share(0, 2)
     landed(va)
     start(vb)
     start(ua[-1])
     start(ua[1])
+    own_tok = pltpu.make_async_copy(tok.at[my_rows], tok.at[my_rows], load_sem.at[1])
+    own_tok.wait()
+    tok_all = remote(tok.at[my_rows], tok.at[sib_rows], tok_sem.at[0], tok_sem.at[1], sibling)
+    tok_all.wait_recv()
+
+    def turn(i):
+        tok_t[i * 256:(i + 1) * 256, :] = tok[:, i * 256:(i + 1) * 256].T
+
+    turn(0)
     landed(zzs[0])
     start(zzs[1])
-    share(2, 4)
+    turn(1)
     landed(ua[0])
     start(ub[0])
     landed(vb)
     start(ua[2])
+    turn(2)
+    turn(3)
     landed(zzs[1])
     start(zzs[2])
-    share(4, 6)
     landed(ua[-1])
     start(ub[-1])
+    turn(4)
     landed(ua[1])
     start(ub[1])
+    turn(5)
     landed(zzs[2])
     start(zzs[3])
-    share(6, 16)
+    turn(6)
     landed(ua[2])
     start(ub[2])
-    own_tok = pltpu.make_async_copy(tok.at[my_rows], tok.at[my_rows], load_sem.at[1])
-    own_tok.wait()
-    tok_all = remote(tok.at[my_rows], tok.at[sib_rows], tok_sem.at[0], tok_sem.at[1], sibling)
-    tok_all.wait_recv()
+    turn(7)
     for r in rels:
         landed(ub[r])
     landed(zzs[3])
 
     def part_copy(n):
-        return remote(part_send.at[n], part_recv.at[n], part_ssem.at[n], part_rsem.at[n], sibling)
+        return remote(part.at[n, sib_rows], part_recv.at[n], part_ssem.at[n], part_rsem.at[n], sibling)
 
     def project(n):
         for kind in range(2):
@@ -227,9 +222,8 @@
                     cols, row = slice(k * 128, (k + 1) * 128), kind * 128
                     head_weight[row:row + MAIN, cols] = gathered[wu, wv, wz]
                     head_weight[row + MAIN:row + 128, cols] = gathered_z[wz, wu, wv]
-        part_send[n] = lax.dot_general(tok[sib_rows, :], head_weight[...], NT, preferred_element_type=F32)
+        part[n] = lax.dot_general(tok[...], head_weight[...], NT, preferred_element_type=F32)
         part_copy(n).start()
-        part_own[n] = lax.dot_general(tok[my_rows, :], head_weight[...], NT, preferred_element_type=F32)
 
     def attend(n, p):
         base = pl.multiple_of((n * 2 + p) * 512, 512)
@@ -275,66 +269,70 @@
             d_kv[rows, :128] += sum(d_keys[j][rows] for j in range(t, 3))
             d_kv[rows, 128:] += sum(d_values[j][rows] for j in range(t, 3))
 
-    def dkv_copies(n):
-        here, there = d_kv_t.at[n, :, my_rows], far_kv_t.at[n, :, my_rows]
-        return [
-            remote(here, here, dkv_ssem.at[n, 0], dkv_rsem.at[n, 0], sibling),
-            remote(here, there, dkv_ssem.at[n, 1], dkv_rsem.at[n, 1], partner[0]),
-            remote(there, there, dkv_ssem.at[n, 2], dkv_rsem.at[n, 2], sibling),
-        ]
-
-    def forward(n):
-        copies = dkv_copies(n)
-        copies[1].wait_recv()
-        copies[2].start()
+    def dkv_copy(n):
+        here = d_kv_t.at[n, my_rows]
+        return remote(here, here, dkv_ssem.at[n], dkv_rsem.at[n], sibling)
 
     def gradient(n):
-        copies = dkv_copies(n)
-        copies[0].wait_recv()
-        if n == 0:
-            for core in range(2):
-                rows = far_tok.at[my_rows if core == 0 else sib_rows]
-                remote(rows, rows, far_send.at[core], far_recv.at[core], partner[core]).wait_recv()
-        copies[2].wait_recv()
-        near, far = d_kv_t[n], far_kv_t[n]
-
-        @pl.loop(0, 4)
-        def _(gz):
-            cols = pl.ds(pl.multiple_of((2 * gz + z_odd) * 256, 256), 256)
-            far_cols = pl.ds(pl.multiple_of(gz * 256, 256), 256)
-            block = jnp.dot(near, tok[:, cols], preferred_element_type=F32)
-            block += jnp.dot(far, far_tok[:, far_cols], preferred_element_type=F32)
-            for kind in range(2):
-                for q in range(4):
-                    for x_hi in range(2):
-                        gx, gy = 2 * x_hi + q % 2, 2 * kind + q // 2
-                        gu, gv = gx + c * (gy - gx), gy + c * (gx - gy)
-                        row = kind * 128 + q * 32
-                        acc[n, gu, gv, gz] = block[row:row + 32, x_hi * 128:(x_hi + 1) * 128]
-
-    def u_halves(n):
-        far = (u + 2) % 4
-        return [
-            remote(acc.at[n, far, :, pl.ds(2 * i, 2)], u_half.at[n, i], u_ssem.at[n, i], u_rsem.at[n, i], u_dev(1 + 2 * i))
+        dkv_copy(n).wait_recv()
+        rhs = d_kv_t[n]
+
+        @pl.loop(0, 2)
+        def _(part_of):
+            lhs = tok_t[pl.ds(pl.multiple_of(part_of * 1024, 1024), 1024), :]
+            block = jnp.dot(lhs, rhs, preferred_element_type=F32)
+            for step in range(4):
+                gz = part_of * 4 + step
+                for kind in range(2):
+                    for q in range(4):
+                        for x_hi in range(2):
+                            gx, gy = 2 * x_hi + q % 2, 2 * kind + q // 2
+                            gu, gv = gx + c * (gy - gx), gy + c * (gx - gy)
+                            row = step * 256 + x_hi * 128 + q * 32
+                            piece = block[row:row + 32, kind * 128:(kind + 1) * 128]
+                            if n == 0:
+                                zacc[gz, gu, gv] = piece
+                            else:
+                                acc[n, gu, (gv - v + 6) % 4, gz] = piece
+
+    slices = (slice(0, 1), slice(1, 4))
+
+    def u_halves(n, part):
+        far, rows = (u + 2) % 4, pl.ds(part, 1 + 2 * part)
+        return [
+            remote(
+                acc.at[n, far, rows, pl.ds(4 * i, 4)], u_half.at[n, i, rows],
+                u_ssem.at[n, 4 * part + i], u_rsem.at[n, 4 * part + i], u_dev(1 + 2 * i),
+            )
             for i in range(2)
         ]
 
-    def u_fulls(n):
-        return [
-            remote(acc.at[n, (u + 1 + 2 * i) % 4], u_full.at[n, i], u_ssem.at[n, 2 + i], u_rsem.at[n, 2 + i], u_dev(1 + 2 * i))
+    def u_fulls(n, part):
+        rows = pl.ds(part, 1 + 2 * part)
+        return [
+            remote(
+                acc.at[n, (u + 1 + 2 * i) % 4, rows], u_full.at[n, i, rows],
+                u_ssem.at[n, 4 * part + 2 + i], u_rsem.at[n, 4 * part + 2 + i], u_dev(1 + 2 * i),
+            )
             for i in range(2)
         ]
 
-    def v_all(n):
-        return [
-            remote(acc.at[n, u, (v + k) % 4], v_recv.at[n, k - 1], v_ssem.at[n, k - 1], v_rsem.at[n, k - 1], v_dev(k))
-            for k in range(1, 4)
+    def v_halves(n):
+        return [
+            remote(acc.at[n, u, 0, pl.ds(4 * i, 4)], v_half.at[n, i], v_ssem.at[n, i], v_rsem.at[n, i], v_dev(1 + 2 * i))
+            for i in range(2)
+        ]
+
+    def v_fulls(n):
+        return [
+            remote(acc.at[n, u, 3 - 2 * i], v_full.at[n, i], v_ssem.at[n, 2 + i], v_rsem.at[n, 2 + i], v_dev(1 + 2 * i))
+            for i in range(2)
         ]
 
     def z_all(n):
         return [
-            remote(acc.at[n, u, v, (z_half + k) % 4], z_recv.at[n, k - 1], z_ssem.at[n, k - 1], z_rsem.at[n, k - 1], z_dev(2 * k))
-            for k in range(1, 4)
+            remote(acc.at[n, u, 2, (z + k) % 8], z_recv.at[n, k - 1], z_ssem.at[n, k - 1], z_rsem.at[n, k - 1], z_dev(k))
+            for k in range(1, 8)
         ]
 
     def to_owner(n):
@@ -342,38 +340,44 @@
         return remote(done.at[n], owned.at[quad], own_ssem.at[n], own_rsem.at[quad], there)
 
     def stage0(n):
-        start(u_halves(n))
-
-    def stage1(n):
-        copies = u_halves(n)
+        start(u_halves(n, 0))
+        start(u_halves(n, 1))
+
+    def stage1(n, part):
+        copies = u_halves(n, part)
         landed(copies)
         for i in range(2):
             near = (u + 1 + 2 * i) % 4
-            for b in range(4):
-                acc[n, near, b, pl.ds(2 * i, 2)] += u_half[n, i, b]
-        start(u_fulls(n))
-        sent(copies)
-
-    def stage2(n):
-        copies = u_fulls(n)
-        landed(copies)
-        for b in range(4):
+            for b in range(*slices[part].indices(4)):
+                acc[n, near, b, pl.ds(4 * i, 4)] += u_half[n, i, b]
+        start(u_fulls(n, part))
+        sent(copies)
+
+    def stage2(n, part):
+        copies = u_fulls(n, part)
+        landed(copies)
+        for b in range(*slices[part].indices(4)):
             acc[n, u, b] += u_full[n, 0, b] + u_full[n, 1, b]
-        start(v_all(n))
+        if part == 0:
+            start(v_halves(n))
         sent(copies)
 
     def stage3(n):
-        copies = v_all(n)
-        landed(copies)
-        acc[n, u, v] += (v_recv[n, 0] + v_recv[n, 1]) + v_recv[n, 2]
+        copies = v_halves(n)
+        landed(copies)
+        for i in range(2):
+            acc[n, u, 3 - 2 * i, pl.ds(4 * i, 4)] += v_half[n, i]
+        start(v_fulls(n))
+        sent(copies)
+
+    def stage4(n):
+        copies = v_fulls(n)
+        landed(copies)
+        acc[n, u, 2] += v_full[n, 0] + v_full[n, 1]
         start(z_all(n))
         sent(copies)
 
-    def stage4(n):
-        copies = z_all(n)
-        landed(copies)
-        total = (acc[n, u, v, z_half] + z_recv[n, 0]) + (z_recv[n, 1] + z_recv[n, 2])
-
+    def hand_over(n, total):
         @pl.when(quad == n)
         def _():
             owned[quad] = total
@@ -383,6 +387,83 @@
             done[n] = total
             to_owner(n).start()
 
+    def stage5(n):
+        copies = z_all(n)
+        landed(copies)
+        total = acc[n, u, 2, z]
+        for k in range(7):
+            total = total + z_recv[n, k]
+        hand_over(n, total)
+        sent(copies)
+
+    def ring_halves():
+        far = (z + 4) % 8
+        return [
+            remote(zacc.at[far, pl.ds(2 * i, 2)], z_half.at[i], zr_send.at[i], zr_recv.at[i], z_dev(1 + 6 * i))
+            for i in range(2)
+        ]
+
+    def ring_fulls(hop):
+        return [
+            remote(
+                zacc.at[(z + (hop if i == 0 else 8 - hop)) % 8], z_full.at[3 - hop, i],
+                zr_send.at[2 * (4 - hop) + i], zr_recv.at[2 * (4 - hop) + i], z_dev(1 + 6 * i),
+            )
+            for i in range(2)
+        ]
+
+    def ring_u():
+        return [
+            remote(zacc.at[z, (u + k) % 4], zu_recv.at[k - 1], zr_send.at[7 + k], zr_recv.at[7 + k], u_dev(k))
+            for k in range(1, 4)
+        ]
+
+    def ring_v():
+        return [
+            remote(zacc.at[z, u, (v + k) % 4], zv_recv.at[k - 1], zr_send.at[10 + k], zr_recv.at[10 + k], v_dev(k))
+            for k in range(1, 4)
+        ]
+
+    def ring0():
+        start(ring_halves())
+
+    def ring1():
+        copies = ring_halves()
+        landed(copies)
+        for i in range(2):
+            zacc[(z + 3 + 2 * i) % 8, pl.ds(2 * i, 2)] += z_half[i]
+        start(ring_fulls(3))
+        sent(copies)
+
+    def ring2(hop):
+        copies = ring_fulls(hop + 1)
+        landed(copies)
+        for i in range(2):
+            near = (z + (hop if i == 0 else 8 - hop)) % 8
+            for b in range(4):
+                zacc[near, b] += z_full[2 - hop, i, b]
+        start(ring_fulls(hop))
+        sent(copies)
+
+    def ring4():
+        copies = ring_fulls(1)
+        landed(copies)
+        for b in range(4):
+            zacc[z, b] += z_full[2, 0, b] + z_full[2, 1, b]
+        start(ring_u())
+        sent(copies)
+
+    def ring5():
+        copies = ring_u()
+        landed(copies)
+        zacc[z, u] += (zu_recv[0] + zu_recv[1]) + zu_recv[2]
+        start(ring_v())
+        sent(copies)
+
+    def ring6():
+        copies = ring_v()
+        landed(copies)
+        hand_over(0, (zacc[z, u, v] + zv_recv[0]) + (zv_recv[1] + zv_recv[2]))
         sent(copies)
 
     def out_copy(n):
@@ -396,7 +477,7 @@
 
     def head(n):
         part_copy(n).wait_recv()
-        kv[...] = (part_own[n] + part_recv[n]).astype(BF16)
+        kv[...] = (part[n, my_rows] + part_recv[n]).astype(BF16)
         d_kv[...] = jnp.zeros_like(d_kv)
 
         def half(p, _):
@@ -405,43 +486,50 @@
 
         lax.fori_loop(0, 2, half, 0)
         out_copy(n).start()
-        d_kv_t[n, :, my_rows] = d_kv[...].astype(BF16).T
-        start(dkv_copies(n)[:2])
-        if n + 2 < KV_HEADS:
-            project(n + 2)
+        d_kv_t[n, my_rows] = d_kv[...].astype(BF16)
+        dkv_copy(n).start()
 
     head(0)
+    project(2)
+    gradient(0)
+    ring0()
     head(1)
-    forward(0)
-    gradient(0)
-    stage0(0)
-    head(2)
-    forward(1)
-    stage1(0)
+    ring1()
+    project(3)
     gradient(1)
     stage0(1)
-    head(3)
-    forward(2)
-    stage1(1)
-    stage2(0)
+    head(2)
+    stage1(1, 0)
+    stage1(1, 1)
+    ring2(2)
     gradient(2)
     stage0(2)
-    forward(3)
-    stage3(0)
-    stage2(1)
+    head(3)
+    stage1(2, 0)
+    stage1(2, 1)
     gradient(3)
     stage0(3)
-    stage1(2)
+    stage2(1, 0)
+    ring2(1)
+    stage2(1, 1)
+    stage1(3, 0)
+    stage2(2, 0)
     stage3(1)
-    stage4(0)
-    stage1(3)
-    stage2(2)
+    stage1(3, 1)
+    stage2(2, 1)
+    stage3(2)
+    ring4()
+    stage2(3, 0)
     stage4(1)
-    stage3(2)
-    stage2(3)
     stage4(2)
+    stage2(3, 1)
     stage3(3)
+    ring5()
+    stage5(1)
+    stage5(2)
     stage4(3)
+    ring6()
+    stage5(3)
 
     for q in range(4):
 
@@ -450,8 +538,7 @@
             to_owner(q).wait_send()
             remote(done.at[q], owned.at[q], own_ssem.at[q], own_rsem.at[q], sibling).wait_recv()
 
-    for q in range(4):
-        kv_grad[q * 32:(q + 1) * 32, :] = owned[q]
+    kv_grad[...] = jnp.concatenate([owned[q] for q in range(4)], axis=0).T
     for k in range(1, 8):
         remote(mine, mine, ag_send.at[k], ag_recv.at[k], z_dev(k)).wait_send()
     sent(va)
@@ -464,12 +551,9 @@
     for copies in zzs:
         sent(copies)
     tok_all.wait_send()
-    for core in range(2):
-        rows = far_tok.at[my_rows]
-        remote(rows, rows, far_send.at[core], far_recv.at[core], partner[core]).wait_send()
     for n in range(KV_HEADS):
         part_copy(n).wait_send()
-        sent(dkv_copies(n))
+        dkv_copy(n).wait_send()
         out_copy(n).wait()
 
 
@@ -487,27 +571,31 @@
         out_specs=(anywhere, pl.BlockSpec(memory_space=vmem)),
         scratch_shapes=[
             vmem((2 * SEQ, HALF), BF16),
-            vmem((2 * SEQ, HALF // 2), BF16),
+            vmem((HALF, 2 * SEQ), BF16),
             vmem((SEQ, WIDTH), BF16),
             vmem((SEQ, WIDTH), BF16),
             vmem((SEQ, WIDTH), BF16),
             vmem((4, 4, 8, MAIN, 128), BF16),
             vmem((8, 4, 4, 128 - MAIN, 128), BF16),
             vmem((256, HALF), BF16),
-            vmem((4, SEQ, 256), F32),
-            vmem((4, SEQ, 256), F32),
+            vmem((4, 2 * SEQ, 256), F32),
             vmem((4, SEQ, 256), F32),
             vmem((SEQ, 256), BF16),
             vmem((SEQ, 256), F32),
-            vmem((4, 256, 2 * SEQ), BF16),
-            vmem((4, 256, 2 * SEQ), BF16),
-            vmem((4, 4, 4, 4, 32, 128), F32),
-            vmem((4, 2, 4, 2, 32, 128), F32),
+            vmem((4, 2 * SEQ, 256), BF16),
+            vmem((4, 4, 4, 8, 32, 128), F32),
             vmem((4, 2, 4, 4, 32, 128), F32),
-            vmem((4, 3, 4, 32, 128), F32),
-            vmem((4, 3, 32, 128), F32),
+            vmem((4, 2, 4, 8, 32, 128), F32),
+            vmem((4, 2, 4, 32, 128), F32),
+            vmem((4, 2, 8, 32, 128), F32),
+            vmem((4, 7, 32, 128), F32),
             vmem((4, 32, 128), F32),
             vmem((4, 32, 128), F32),
+            vmem((8, 4, 4, 32, 128), F32),
+            vmem((2, 2, 4, 32, 128), F32),
+            vmem((3, 2, 4, 4, 32, 128), F32),
+            vmem((3, 4, 32, 128), F32),
+            vmem((3, 32, 128), F32),
             dma((5,)),
             dma((2,)),
             dma((28,)),
@@ -516,16 +604,16 @@
             dma((15,)),
             dma((4,)),
             dma((4,)),
-            dma((4, 3)),
-            dma((4, 3)),
-            dma((2,)),
-            dma((2,)),
+            dma((4,)),
+            dma((4,)),
+            dma((14,)),
+            dma((14,)),
+            dma((4, 8)),
+            dma((4, 8)),
             dma((4, 4)),
             dma((4, 4)),
-            dma((4, 3)),
-            dma((4, 3)),
-            dma((4, 3)),
-            dma((4, 3)),
+            dma((4, 7)),
+            dma((4, 7)),
             dma((4,)),
             dma((4,)),
             dma((4,)),

time: 122 us -> 113 us (0.926)
  Pallas kernels: 116 us -> 108 us
    pallas_call x1, Pallas kernels: 116 us -> 108 us  [on_device(): pl.pallas_call(kernel, out_shape=(jax.ShapeDtypeStruct((SEQ, WIDTH), BF16...]
where the time goes in v3:
time: 113 us
  Pallas kernels  108 us (96%)
  local copies, waits for them, and re-layouts  4.57 us (4%)
    pallas_call x1, Pallas kernels, on_device(): pl.pallas_call(kernel, out_shape=(jax.ShapeDtypeStruct((SEQ, WIDTH), BF16...  108 us
    unnamed x4, local copies, waits for them, and re-layouts  4.57 us

profile of v3, /device:TPU:10, one launch (start us, length us, event | category | flops | bytes accessed | tf_op | source)
XLA Modules:
  0.0 113.1 jit_solution(11577990725037488067)
XLA Ops:
  0.6 107.9 %shard_map.59 = (bf16[384,4096]{1,0:T(8,128)(2,1)}, f32[128,128]{1,0:T(8,128)}) custom-call(bf16[384,4096]{1,0:T(8,128)(2,1)} %tokens.1, bf16[384,4096]{1,0:T(8,128)(2,1)} %queries.1, bf16[128,128]{1,0:T(8,128)(2,1)} %weight.1, bf16[384,4096]{1,0:T(8,128)(2,1)} %cotangent.1), custom_call_target="tpu_custom_call" | custom-call | flops 12000000000 | bytes 16777216 | tf_op jit(solution)/shard_map/pallas_call | solution.py:564
  108.5 0.0 copy-start
  108.5 3.9 %copy.8 = bf16[384,4096]{1,0:T(8,128)(2,1)} copy(bf16[384,4096]{1,0:T(8,128)(2,1)} %get-tuple-element.4) | data formatting | bytes 6291456
  112.4 0.0 copy-done
  112.4 0.6 copy.9
Async XLA Ops:
  108.5 4.0 %copy-start = (f32[128,128]{1,0:T(8,128)S(1)}, f32[128,128]{1,0:T(8,128)}, u32[]{:S(2)}) copy-start(f32[128,128]{1,0:T(8,128)} %get-tuple-element.5) | copy-start | bytes 196612

commit v4 on v3

--- a/solution.py
+++ b/solution.py
@@ -290,7 +290,7 @@
                             gu, gv = gx + c * (gy - gx), gy + c * (gx - gy)
                             row = step * 256 + x_hi * 128 + q * 32
                             piece = block[row:row + 32, kind * 128:(kind + 1) * 128]
-                            if n == 0:
+                            if n == 1:
                                 zacc[gz, gu, gv] = piece
                             else:
                                 acc[n, gu, (gv - v + 6) % 4, gz] = piece
@@ -463,7 +463,7 @@
     def ring6():
         copies = ring_v()
         landed(copies)
-        hand_over(0, (zacc[z, u, v] + zv_recv[0]) + (zv_recv[1] + zv_recv[2]))
+        hand_over(1, (zacc[z, u, v] + zv_recv[0]) + (zv_recv[1] + zv_recv[2]))
         sent(copies)
 
     def out_copy(n):
@@ -490,43 +490,43 @@
         dkv_copy(n).start()
 
     head(0)
+    gradient(0)
+    stage0(0)
     project(2)
-    gradient(0)
+    head(1)
+    stage1(0, 0)
+    stage1(0, 1)
+    gradient(1)
     ring0()
-    head(1)
+    project(3)
+    head(2)
     ring1()
-    project(3)
-    gradient(1)
-    stage0(1)
-    head(2)
-    stage1(1, 0)
-    stage1(1, 1)
-    ring2(2)
+    stage2(0, 0)
+    stage2(0, 1)
     gradient(2)
     stage0(2)
+    stage3(0)
     head(3)
+    stage4(0)
     stage1(2, 0)
     stage1(2, 1)
     gradient(3)
     stage0(3)
-    stage2(1, 0)
-    ring2(1)
-    stage2(1, 1)
+    ring2(2)
+    stage5(0)
     stage1(3, 0)
     stage2(2, 0)
-    stage3(1)
     stage1(3, 1)
     stage2(2, 1)
     stage3(2)
-    ring4()
+    ring2(1)
     stage2(3, 0)
-    stage4(1)
     stage4(2)
     stage2(3, 1)
     stage3(3)
+    ring4()
+    stage5(2)
     ring5()
-    stage5(1)
-    stage5(2)
     stage4(3)
     ring6()
     stage5(3)

time: 113 us -> 113 us (level)
  no operation moved by 1% of the time
where the time goes in v4:
time: 113 us
  Pallas kernels  108 us (96%)
  local copies, waits for them, and re-layouts  4.57 us (4%)
    pallas_call x1, Pallas kernels, on_device(): pl.pallas_call(kernel, out_shape=(jax.ShapeDtypeStruct((SEQ, WIDTH), BF16...  108 us
    unnamed x4, local copies, waits for them, and re-layouts  4.57 us

profile of v4, /device:TPU:10, one launch (start us, length us, event | category | flops | bytes accessed | tf_op | source)
XLA Modules:
  0.0 112.8 jit_solution(8376924656769919211)
XLA Ops:
  0.6 107.6 %shard_map.59 = (bf16[384,4096]{1,0:T(8,128)(2,1)}, f32[128,128]{1,0:T(8,128)}) custom-call(bf16[384,4096]{1,0:T(8,128)(2,1)} %tokens.1, bf16[384,4096]{1,0:T(8,128)(2,1)} %queries.1, bf16[128,128]{1,0:T(8,128)(2,1)} %weight.1, bf16[384,4096]{1,0:T(8,128)(2,1)} %cotangent.1), custom_call_target="tpu_custom_call" | custom-call | flops 12000000000 | bytes 16777216 | tf_op jit(solution)/shard_map/pallas_call | solution.py:564
  108.2 0.0 copy-start
  108.2 3.9 %copy.8 = bf16[384,4096]{1,0:T(8,128)(2,1)} copy(bf16[384,4096]{1,0:T(8,128)(2,1)} %get-tuple-element.4) | data formatting | bytes 6291456
  112.2 0.0 copy-done
  112.2 0.6 copy.9
Async XLA Ops:
  108.2 4.0 %copy-start = (f32[128,128]{1,0:T(8,128)S(1)}, f32[128,128]{1,0:T(8,128)}, u32[]{:S(2)}) copy-start(f32[128,128]{1,0:T(8,128)} %get-tuple-element.5) | copy-start | bytes 196612
